TPU v7x, 256 devices: a whole 4x4x8 slice. The times are simulated.
256 devices in a mesh: seq: 16 (over z, core), ch: 4 (over x), dp: 4 (over y).
Axes of the slice: x: 4, y: 4, z: 8, core: 2. Of those that a mesh axis runs over, the one named last changes fastest.
Arguments:
- grad_out: bfloat16 [4, 2048, 4096], P('dp', 'seq', 'ch'), may hold values from -6 to 6
- inputs: bfloat16 [4, 2048, 4096], P('dp', 'seq', 'ch'), may hold values from -6 to 6
- decay_rate: float32 [64, 4096], P(None, 'ch'), may hold values from 0.01 to 103
- frequency: float32 [64, 4096], P(None, 'ch'), may hold values from -3.140625 to 3.140625
- in_proj: float32 [2, 64, 4096], P(None, None, 'ch'), may hold values from -6 to 6
- out_proj: float32 [2, 64, 4096], P(None, None, 'ch'), may hold values from -0.015625 to 0.015625
- skip_gain: float32 [4096], P('ch'), may hold values from 0.1 to 1.9
- doc_lengths: int32 [4, 4], P('dp'), may hold values from 1 to 1024, 2048 in all within a row
- piece_lengths: int32 [4, 16, 4], P('dp', 'seq'), may hold values from 1 to 64, 128 in all within a row
Outputs:
- returned: bfloat16 [16, 4, 4, 64, 4096], P('seq', 'dp', None, None, 'ch')
- grad_b: float32 [2, 64, 4096], P(None, None, 'ch')
Inputs may be any that keep to these rules, and one draw needn't show every extreme that they name: `doc_lengths`: the lengths of a row sum to 2048, and the largest is exactly 1024. `piece_lengths`: the lengths of one row and index of seq sum to 128, and the largest is exactly 64.
All inputs are finite; a program needn't handle non-finite values.
Results may differ from a plain program's by a relative error of at most 0.0013.
Values may be sent and summed in bfloat16 or wider, within the bound.
A program may use at most 128 MiB of HBM per device.

v0:
```python
import math

import jax
import jax.numpy as jnp
from jax import lax
from jax.sharding import PartitionSpec as P

exact_precision = lax.Precision.HIGHEST


def from_behind(value, axis, steps):
    count = lax.axis_size(axis)
    initial, last = (max(0, -steps), min(count, count - steps))
    return lax.ppermute(value, axis, [(source, source + steps) for source in range(initial, last)])


def mode_powers(step_rate, frequency, lag_count):
    lagged = jnp.arange(lag_count, dtype=jnp.float32)[:, None, None]
    decay_pow = jnp.exp(-lagged * step_rate[None])
    phases = lagged * frequency[None]
    return jnp.concatenate([decay_pow * jnp.cos(phases), -decay_pow * jnp.sin(phases)], axis=1)


def complex_mul(first_re, first_im, second_re, second_im):
    return (
        first_re * second_re - first_im * second_im,
        first_re * second_im + first_im * second_re,
    )


def shards(
    grad_out,
    inputs,
    decay_rate,
    frequency,
    in_proj,
    out_proj,
    skip_gain,
    doc_lengths,
    piece_lengths,
):
    length = grad_out.shape[1]
    channels = grad_out.shape[2]
    mode_count = decay_rate.shape[0]
    seq_count = lax.axis_size("seq")
    row_count = lax.axis_size("dp")
    seq_length = length * seq_count
    block_len = min(32, length)
    block_count = length // block_len
    group_width = math.gcd(channels, 128)
    group_count = channels // group_width
    step_rate = decay_rate / seq_length
    position = lax.axis_index("seq") * length + jnp.arange(length, dtype=jnp.int32)
    boundary = jnp.cumsum(doc_lengths[0])[:-1]
    is_start = jnp.any(position[:, None] == boundary[None, :], axis=1)
    keep_mask = jnp.where(is_start, 0.0, 1.0).astype(jnp.float32)
    segment = jnp.sum((boundary[None, :] <= position[:, None]).astype(jnp.int32), axis=1).reshape(
        block_count, block_len
    )
    lag_index = jnp.arange(block_len)[:, None] + jnp.arange(block_len)[None, :]
    in_block = lag_index < block_len
    lag_clip = jnp.minimum(lag_index, block_len - 1)
    same_doc = segment[:, :, None] == segment[:, lag_clip]
    lag_mask = jnp.where(same_doc & in_block[None], 1.0, 0.0).astype(jnp.float32)
    closing = jnp.where(segment == segment[:, -1:], 1.0, 0.0).astype(jnp.float32)
    first_keep = keep_mask.reshape(block_count, block_len)[:, 0]
    lead_value = first_keep * closing[:, 0]
    grad_rows = grad_out[0].reshape(block_count, block_len, channels)
    input_rows = inputs[0].reshape(block_count, block_len, channels)
    weight_re = in_proj[0] * out_proj[0] + in_proj[1] * out_proj[1]
    weight_im = in_proj[0] * out_proj[1] - in_proj[1] * out_proj[0]
    weight_cat = jnp.concatenate([weight_re, -weight_im], axis=0)
    group_ids = jnp.arange(group_count, dtype=jnp.int32)

    def pick_group(source, group_id):
        return lax.dynamic_slice_in_dim(
            source, group_id * group_width, group_width, source.ndim - 1
        )

    def local_group(group_id):
        powers = mode_powers(
            pick_group(step_rate, group_id), pick_group(frequency, group_id), block_len + 1
        )
        kernel = jnp.einsum(
            "kmc,mc->kc",
            powers[:block_len],
            pick_group(weight_cat, group_id),
            precision=exact_precision,
        )
        grad_group = pick_group(grad_rows, group_id).astype(jnp.float32)
        input_group = pick_group(input_rows, group_id).astype(jnp.float32)
        shifted = grad_group[:, lag_clip, :] * lag_mask[..., None]
        local_du = jnp.einsum("jtkc,kc->jtc", shifted, kernel, precision=exact_precision)
        lagged = jnp.einsum("jtkc,jtc->kc", shifted, input_group, precision=exact_precision)
        head_rows = jnp.concatenate([lagged, jnp.zeros((1, group_width), jnp.float32)], axis=0)[
            None
        ]
        leading = jnp.concatenate(
            [
                jnp.zeros((block_count, 1, group_width), jnp.float32),
                first_keep[:, None, None] * shifted[:, 0],
            ],
            axis=1,
        )
        closing_rows = (input_group * closing[:, :, None])[:, ::-1, :]
        trailing = jnp.concatenate(
            [closing_rows, jnp.zeros((block_count, 1, group_width), jnp.float32)], axis=1
        )
        stacked = jnp.concatenate([head_rows, leading, trailing], axis=0)
        moments = jnp.einsum("kmc,vkc->vmc", powers, stacked, precision=exact_precision)
        return (local_du, moments)

    local_du, moments = lax.map(local_group, group_ids)
    local_du = jnp.moveaxis(local_du, 0, 2).reshape(length, channels)
    moments = jnp.moveaxis(moments, 0, 2).reshape(moments.shape[1], 2 * mode_count, channels)
    moment_re = moments[:, :mode_count]
    moment_im = moments[:, mode_count:]
    proj_re = out_proj[0]
    proj_im = out_proj[1]
    own_re, own_im = complex_mul(proj_re, proj_im, moment_re[0], moment_im[0])
    push_re, push_im = complex_mul(
        proj_re[None], proj_im[None], moment_re[1 : 1 + block_count], moment_im[1 : 1 + block_count]
    )
    tail_re = moment_re[1 + block_count :]
    tail_im = moment_im[1 + block_count :]
    full_decay = jnp.exp(-block_len * step_rate)
    power_re = full_decay * jnp.cos(block_len * frequency)
    power_im = -full_decay * jnp.sin(block_len * frequency)

    def compose_block(carried, block_input):
        factor, push_block_re, push_block_im = block_input
        total_re, total_im = complex_mul(
            factor * power_re, factor * power_im, carried[0], carried[1]
        )
        shift_re, shift_im = complex_mul(
            factor * power_re, factor * power_im, carried[2], carried[3]
        )
        return ((total_re, total_im, shift_re + push_block_re, shift_im + push_block_im), None)

    blank = jnp.zeros((mode_count, channels), jnp.float32)
    summary, unused = lax.scan(
        compose_block,
        (jnp.ones_like(blank), blank, blank, blank),
        (lead_value, push_re, push_im),
        reverse=True,
    )
    total_re, total_im, shift_re, shift_im = summary

    def relay_step(step_id, incoming):
        out_re, out_im = complex_mul(total_re, total_im, incoming[0], incoming[1])
        return from_behind((out_re + shift_re, out_im + shift_im), "seq", -1)

    entry_re, entry_im = lax.fori_loop(0, seq_count - 1, relay_step, (blank, blank))

    def enter_block(incoming, block_input):
        factor, push_block_re, push_block_im = block_input
        out_re, out_im = complex_mul(factor * power_re, factor * power_im, incoming[0], incoming[1])
        return ((out_re + push_block_re, out_im + push_block_im), incoming)

    final_state, entries = lax.scan(
        enter_block, (entry_re, entry_im), (lead_value, push_re, push_im), reverse=True
    )
    carry_re, carry_im = complex_mul(entries[0], entries[1], tail_re, tail_im)
    grad_re = own_re + jnp.sum(carry_re, axis=0)
    grad_im = own_im + jnp.sum(carry_im, axis=0)
    reduced = lax.psum((grad_re, grad_im), ("seq", "dp"))
    grad_scale = math.sqrt(mode_count / (row_count * seq_length))
    grad_b = jnp.stack([reduced[0], reduced[1]]) * grad_scale
    mix_re = in_proj[0][None] * entries[0] + in_proj[1][None] * entries[1]
    mix_im = in_proj[0][None] * entries[1] - in_proj[1][None] * entries[0]
    mix_cat = jnp.concatenate([mix_re, -mix_im], axis=1)

    def carry_group(group_id):
        powers = mode_powers(
            pick_group(step_rate, group_id), pick_group(frequency, group_id), block_len
        )
        return jnp.einsum(
            "kmc,jmc->jkc", powers, pick_group(mix_cat, group_id), precision=exact_precision
        )

    carried = jnp.moveaxis(lax.map(carry_group, group_ids), 0, 2)[:, ::-1]
    carried = (carried * closing[:, :, None, None]).reshape(length, channels)
    input_grad = (local_du + carried + skip_gain[None] * grad_out[0].astype(jnp.float32)).astype(
        jnp.bfloat16
    )
    lengths_row = piece_lengths[0, 0]
    offsets = jnp.cumsum(lengths_row) - lengths_row
    most_rows = length // 2
    slot_ids = jnp.arange(most_rows, dtype=jnp.int32)
    row_index = jnp.minimum(offsets[:, None] + slot_ids[None, :], length - 1)
    in_piece = slot_ids[None, :] < lengths_row[:, None]
    outgoing = jnp.where(in_piece[:, :, None], input_grad[row_index], jnp.zeros((), jnp.bfloat16))
    returned = lax.all_to_all(outgoing, "dp", split_axis=0, concat_axis=0, tiled=True)
    return (returned[None, None], grad_b)


def solution(mesh):
    return jax.shard_map(
        shards,
        mesh=mesh,
        in_specs=(
            P("dp", "seq", "ch"),
            P("dp", "seq", "ch"),
            P(None, "ch"),
            P(None, "ch"),
            P(None, None, "ch"),
            P(None, None, "ch"),
            P("ch"),
            P("dp", None),
            P("dp", "seq", None),
        ),
        out_specs=(P("seq", "dp", None, None, "ch"), P(None, None, "ch")),
        check_vma=False,
    )
```

profile of v0, /device:TPU:1, one launch (start us, length us, event | category | flops | bytes accessed | tf_op | source)
XLA Modules:
  0.0 889.6 jit_solution(4392224181891225417)
XLA Ops:
  25.2 297.4 %while.79 = (s32[]{:T(128)}, f32[8,4,32,128]{3,2,1,0:T(8,128)}, f32[8,9,128,128]{2,1,3,0:T(8,128)}, s32[8]{0:T(128)}, f32[128,1024]{1,0:T(8,128)}, /*index=5*/f3...) while((s32[]{:T(128)}, f32[8,4,32,128]{3,2,1,0:T(8,128)}, ...), condition=%wide.region_4.5_spmd.clone, body=%wide.region_3.4_spmd.clone.sunk | while | flops 70093864 | bytes 31301156 | solution.py:113
  36.0 9.6 %cosine_multiply_fusion.6 = (f32[33,64,128]{1,0,2:T(8,128)S(1)}, f32[33,64,128]{1,0,2:T(8,128)S(1)}) fusion(f32[64,128]{0,1:T(8,128)S(1)} %get-tuple-element.1160, f32[64,128]{0,1:T(8,128)S(1)} %get-tuple-element.1161, f32[33]{0:T(128)S(1)} %iota_negate_fusion.5), kind=kLoop, calls=%fused_computation.34.clone.1 | loop fusion | flops 1351680 | bytes 2228356 | tf_op jit(solution)/shard_map/while/body/eval_jaxpr/mul | solution.py:21
  56.7 5.7 fusion.61
  73.2 9.6 %cosine_multiply_fusion.6 = (f32[33,64,128]{1,0,2:T(8,128)S(1)}, f32[33,64,128]{1,0,2:T(8,128)S(1)}) fusion(f32[64,128]{0,1:T(8,128)S(1)} %get-tuple-element.1160, f32[64,128]{0,1:T(8,128)S(1)} %get-tuple-element.1161, f32[33]{0:T(128)S(1)} %iota_negate_fusion.5), kind=kLoop, calls=%fused_computation.34.clone.1 | loop fusion | flops 1351680 | bytes 2228356 | tf_op jit(solution)/shard_map/while/body/eval_jaxpr/mul | solution.py:21
  93.8 5.7 fusion.61
  110.3 9.6 %cosine_multiply_fusion.6 = (f32[33,64,128]{1,0,2:T(8,128)S(1)}, f32[33,64,128]{1,0,2:T(8,128)S(1)}) fusion(f32[64,128]{0,1:T(8,128)S(1)} %get-tuple-element.1160, f32[64,128]{0,1:T(8,128)S(1)} %get-tuple-element.1161, f32[33]{0:T(128)S(1)} %iota_negate_fusion.5), kind=kLoop, calls=%fused_computation.34.clone.1 | loop fusion | flops 1351680 | bytes 2228356 | tf_op jit(solution)/shard_map/while/body/eval_jaxpr/mul | solution.py:21
  131.0 5.7 fusion.61
  147.5 9.6 %cosine_multiply_fusion.6 = (f32[33,64,128]{1,0,2:T(8,128)S(1)}, f32[33,64,128]{1,0,2:T(8,128)S(1)}) fusion(f32[64,128]{0,1:T(8,128)S(1)} %get-tuple-element.1160, f32[64,128]{0,1:T(8,128)S(1)} %get-tuple-element.1161, f32[33]{0:T(128)S(1)} %iota_negate_fusion.5), kind=kLoop, calls=%fused_computation.34.clone.1 | loop fusion | flops 1351680 | bytes 2228356 | tf_op jit(solution)/shard_map/while/body/eval_jaxpr/mul | solution.py:21
  168.2 5.7 fusion.61
  184.7 9.6 %cosine_multiply_fusion.6 = (f32[33,64,128]{1,0,2:T(8,128)S(1)}, f32[33,64,128]{1,0,2:T(8,128)S(1)}) fusion(f32[64,128]{0,1:T(8,128)S(1)} %get-tuple-element.1160, f32[64,128]{0,1:T(8,128)S(1)} %get-tuple-element.1161, f32[33]{0:T(128)S(1)} %iota_negate_fusion.5), kind=kLoop, calls=%fused_computation.34.clone.1 | loop fusion | flops 1351680 | bytes 2228356 | tf_op jit(solution)/shard_map/while/body/eval_jaxpr/mul | solution.py:21
  205.4 5.7 fusion.61
  221.8 9.6 %cosine_multiply_fusion.6 = (f32[33,64,128]{1,0,2:T(8,128)S(1)}, f32[33,64,128]{1,0,2:T(8,128)S(1)}) fusion(f32[64,128]{0,1:T(8,128)S(1)} %get-tuple-element.1160, f32[64,128]{0,1:T(8,128)S(1)} %get-tuple-element.1161, f32[33]{0:T(128)S(1)} %iota_negate_fusion.5), kind=kLoop, calls=%fused_computation.34.clone.1 | loop fusion | flops 1351680 | bytes 2228356 | tf_op jit(solution)/shard_map/while/body/eval_jaxpr/mul | solution.py:21
  242.5 5.7 fusion.61
  259.0 9.6 %cosine_multiply_fusion.6 = (f32[33,64,128]{1,0,2:T(8,128)S(1)}, f32[33,64,128]{1,0,2:T(8,128)S(1)}) fusion(f32[64,128]{0,1:T(8,128)S(1)} %get-tuple-element.1160, f32[64,128]{0,1:T(8,128)S(1)} %get-tuple-element.1161, f32[33]{0:T(128)S(1)} %iota_negate_fusion.5), kind=kLoop, calls=%fused_computation.34.clone.1 | loop fusion | flops 1351680 | bytes 2228356 | tf_op jit(solution)/shard_map/while/body/eval_jaxpr/mul | solution.py:21
  279.7 5.7 fusion.61
  296.2 9.6 %cosine_multiply_fusion.6 = (f32[33,64,128]{1,0,2:T(8,128)S(1)}, f32[33,64,128]{1,0,2:T(8,128)S(1)}) fusion(f32[64,128]{0,1:T(8,128)S(1)} %get-tuple-element.1160, f32[64,128]{0,1:T(8,128)S(1)} %get-tuple-element.1161, f32[33]{0:T(128)S(1)} %iota_negate_fusion.5), kind=kLoop, calls=%fused_computation.34.clone.1 | loop fusion | flops 1351680 | bytes 2228356 | tf_op jit(solution)/shard_map/while/body/eval_jaxpr/mul | solution.py:21
  316.9 5.7 fusion.61
  322.6 12.9 %fusion.38 = (f32[4,64,1024]{1,0,2:T(4,128)}, f32[4,64,1024]{1,0,2:T(4,128)S(1)}, f32[4,64,1024]{1,0,2:T(4,128)}, f32[4,64,1024]{1,0,2:T(4,128)}) fusion(f32[9,128,1024]{1,0,2:T(8,128)} %bitcast.207), kind=kLoop, calls=%fused_computation.121 | loop fusion | bytes 8388608 | tf_op jit(solution)/shard_map/slice | solution.py:124
  342.9 10.0 %while.80 = (s32[]{:T(128)}, f32[64,1024]{1,0:T(8,128)S(1)}, f32[64,1024]{1,0:T(8,128)S(1)}, f32[64,1024]{1,0:T(8,128)S(1)}, f32[64,1024]{1,0:T(8,128)S(1)}, /*i...) while((s32[]{:T(128)}, f32[64,1024]{1,0:T(8,128)S(1)}, ...), condition=%wide.region_6.7_spmd.clone, body=%wide.region_5.6_spmd.clone.sunk | while | flops 1310724 | bytes 3145903 | solution.py:141
  353.0 175.0 %while.76 = (s32[]{:T(128)}, f32[64,1024]{1,0:T(8,128)S(1)}, f32[64,1024]{1,0:T(8,128)S(1)}, f32[64,1024]{1,0:T(8,128)S(1)}, f32[64,1024]{1,0:T(8,128)S(1)}, /*i...) while((s32[]{:T(128)}, f32[64,1024]{1,0:T(8,128)S(1)}, f32[64,1024]{1,0:T(8,128)S(1)}, ...), condition=%wide.region_8.9_spmd, body=%wide.region_7.8_spmd.sunk | while | flops 524290 | bytes 4194469 | solution.py:153
  353.8 5.1 collective-permute-start
  530.2 13.0 %while.77 = (s32[]{:T(128)}, f32[64,1024]{1,0:T(8,128)S(1)}, f32[64,1024]{1,0:T(8,128)S(1)}, f32[4,64,1024]{2,1,0:T(8,128)}, f32[4,64,1024]{2,1,0:T(8,128)}, /*i...) while((s32[]{:T(128)}, f32[64,1024]{1,0:T(8,128)S(1)}, ...), condition=%wide.region_10.11_spmd, body=%wide.region_9.10_spmd.sunk | while | flops 655363 | bytes 3145889 | solution.py:160
  551.5 114.8 %while.78 = (s32[]{:T(128)}, f32[8,4,32,128]{3,2,1,0:T(8,128)}, s32[8]{0:T(128)S(1)}, f32[4,128,1024]{2,1,0:T(8,128)S(1)}, f32[64,1024]{0,1:T(8,128)}, /*index=5...) while((s32[]{:T(128)}, f32[8,4,32,128]{3,2,1,0:T(8,128)}, s32[8]{0:T(128)S(1)}, ...), condition=%wide.region_12.13_spmd, body=%wide.region_11.12_spmd.sunk | while | flops 27000868 | bytes 6029747 | solution.py:181
  554.0 7.6 cosine_multiply_fusion.5
  568.3 7.6 cosine_multiply_fusion.5
  582.7 7.6 cosine_multiply_fusion.5
  597.0 7.6 cosine_multiply_fusion.5
  611.3 7.6 cosine_multiply_fusion.5
  625.7 7.6 cosine_multiply_fusion.5
  640.0 7.6 cosine_multiply_fusion.5
  654.4 7.6 cosine_multiply_fusion.5
  682.2 197.9 %all-reduce.6.cloned.1.call-done = (f32[1,64,1024]{2,1,0:T(8,128)}, f32[1,64,1024]{2,1,0:T(8,128)}) async-done(((f32[1,64,1024]{2,1,0:T(8,128)}, f32[1,64,1024]{2,1,0:T(8,128)}), (f32[1,64,1024]{2,1,0:T(8,128)}, f32[1,64,1024]{2,1,0:T(8,128)})) %all-reduce.6.cloned.1.call-update) | async-done | bytes 524304 | tf_op jit(solution)/shard_map/psum | solution.py:166
  (458 shorter events, 464.2 us)
Async XLA Ops:
  353.8 9.2 %collective-permute-start = (f32[64,1024]{1,0:T(8,128)}, f32[64,1024]{1,0:T(8,128)S(1)}, u32[]{:S(2)}, u32[]{:S(2)}) collective-permute-start(f32[64,1024]{1,0:T(8,128)} %get-tuple-element.1119), channel_id=1, source_target_pairs={{16,0},{32,16},{48,32},{64,48},{80,64},{96,80},{112,96},{128,112},... | collective-permute-start | bytes 786440 | tf_op jit(solution)/shard_map/while/body/eval_jaxpr/ppermute | solution.py:14
  359.0 7.7 collective-permute-start.1
  367.5 7.9 collective-permute-start
  369.4 8.8 collective-permute-start.1
  379.0 7.9 collective-permute-start
  380.9 8.8 collective-permute-start.1
  390.5 7.9 collective-permute-start
  392.5 8.8 collective-permute-start.1
  402.1 7.9 collective-permute-start
  404.0 8.8 collective-permute-start.1
  413.6 7.9 collective-permute-start
  415.5 8.8 collective-permute-start.1
  425.1 7.9 collective-permute-start
  427.0 8.8 collective-permute-start.1
  436.6 7.9 collective-permute-start
  438.5 8.8 collective-permute-start.1
  448.1 7.9 collective-permute-start
  450.1 8.8 collective-permute-start.1
  459.7 7.9 collective-permute-start
  461.6 8.8 collective-permute-start.1
  471.2 7.9 collective-permute-start
  473.1 8.8 collective-permute-start.1
  482.7 7.9 collective-permute-start
  484.6 8.8 collective-permute-start.1
  494.2 7.9 collective-permute-start
  496.2 8.8 collective-permute-start.1
  505.8 7.9 collective-permute-start
  507.7 8.8 collective-permute-start.1
  517.3 7.9 collective-permute-start
  519.2 8.8 collective-permute-start.1
  672.2 209.8 %all-to-all-start = ((bf16[4,64,1024]{2,1,0:T(8,128)(2,1)}), bf16[4,64,1024]{2,1,0:T(8,128)(2,1)S(1)}, u32[]{:S(2)}, u32[]{:S(2)}) async-start(bf16[4,64,1024]{2,1,0:T(8,128)(2,1)} %broadcast_select_fusion), calls=%async_computation | async-start | bytes 1048576 | tf_op jit(solution)/shard_map/all_to_all | solution.py:193
  675.7 204.4 %all-reduce.6.cloned.1.call-start = ((), (), s32[]{:S(2)}) async-start(), calls=%async_computation.1 | async-start | bytes 1048576 | tf_op jit(solution)/shard_map/psum | solution.py:166
  (23 other events, 197.8 us)
Sparse Core Ops, SparseCore 0:
  682.3 197.7 all-reduce.5
where the time goes:
time: 896 us; the launch traced here: 890 us
  waiting for transfers between devices  300 us (33%)
  other arithmetic  248 us (28%)
  local copies, waits for them, and re-layouts  150 us (17%)
  matrix products  102 us (11%)
  starting transfers between devices  64.2 us (7%)
  between operations  14.4 us (2%)
  loops' own time  11.5 us (1%)
    psum x1, waiting for transfers between devices, shards(): reduced = lax.psum((grad_re, grad_im), ('seq', 'dp'))  198 us
    mul x16, other arithmetic, mode_powers(): decay_pow * jnp.cos(phases)  138 us
    ppermute x30, waiting for transfers between devices, from_behind(): lax.ppermute(value, axis, [(source, source + steps) for source in range(i...  102 us
    ppermute x30, starting transfers between devices, from_behind(): lax.ppermute(value, axis, [(source, source + steps) for source in range(i...  60.7 us
    dot_general x8, matrix products, local_group(): jnp.einsum('kmc,vkc->vmc', powers, stacked, precision=exact_precision)  45.7 us
    gather x16, local copies, waits for them, and re-layouts, local_group(): shifted = grad_group[:, lag_clip, :] * lag_mask[..., None]  29.5 us
    dot_general x8, matrix products, local_group(): jnp.einsum('kmc,mc->kc', powers[:block_len], pick_group(weight_cat, group...  28 us
    dot_general x8, matrix products, carry_group(): jnp.einsum('kmc,jmc->jkc', powers, pick_group(mix_cat, group_id), precisi...  27.9 us
  transfers between devices with their start and end apart: 32, of which 31 were waited for; matrix products, arithmetic and copies ran while one was open for 1% of the time, Pallas kernels for 0%

commit v1 on v0

v1 whole, which is shorter than its diff:
```python
import math

import jax
import jax.numpy as jnp
from jax import lax
from jax.experimental import pallas as pl
from jax.experimental.pallas import tpu as pltpu
from jax.sharding import PartitionSpec as P

MESH = pl.DeviceIdType.MESH
F32 = jnp.float32
BF16 = jnp.bfloat16
I32 = jnp.int32

SEQ = 16
DP = 4
SETS = 2
LEN = 128
WIDE = 512
LANES = 128
GROUP = 32
QUARTER = 32
MODES = 64
ROWS = 16
UNROLL = 16
LAG = 2


def lane_block():
    return lax.broadcasted_iota(I32, (1, LANES), 1) // GROUP


def turn(tile, blocks):
    shift = (blocks % 4) * GROUP
    return tile if shift == 0 else pltpu.roll(tile, shift, 1)


def swap_blocks(tiles):
    block = lane_block()
    out = []
    for g in range(4):
        acc = turn(tiles[0], -g)
        for b in range(1, 4):
            acc = jnp.where(block == b, turn(tiles[b], b - g), acc)
        out.append(acc)
    return out


def spread_blocks(tile):
    block = lane_block()
    turned = [turn(tile, k) for k in range(4)]
    out = []
    for b in range(4):
        acc = turned[(0 - b) % 4]
        for lane in range(1, 4):
            acc = jnp.where(block == lane, turned[(lane - b) % 4], acc)
        out.append(acc)
    return out


def kernel(
    grad_hbm,
    input_hbm,
    decay_hbm,
    freq_hbm,
    in_hbm,
    out_hbm,
    skip_hbm,
    docs,
    pieces,
    ret_ref,
    gb_ref,
    grad_v,
    input_v,
    param_v,
    skip_v,
    send_a,
    recv_a,
    coef,
    proj,
    skips,
    state,
    total,
    gd,
    ud,
    partial,
    send_d,
    recv_d,
    rows_d,
    pick,
    send_y,
    g_dp,
    g_seq,
    load_sem,
    a_send,
    a_recv,
    d_send,
    d_recv,
    y_send,
    y_recv,
    p_send,
    p_recv,
    s_send,
    s_recv,
    c_send,
    c_recv,
):
    me = lax.axis_index("seq")
    row = lax.axis_index("dp")
    core = lax.rem(me, 2)
    chip = me // 2
    block = lane_block()
    own_block = lax.rem(me, 4)

    loads = []

    def load(src, dst):
        copy = pltpu.make_async_copy(src, dst, load_sem.at[len(loads)])
        copy.start()
        loads.append(copy)

    for c in range(SETS):
        wide = pl.ds(c * WIDE, WIDE)
        load(grad_hbm.at[0, :, wide], grad_v.at[c])
        load(input_hbm.at[0, :, wide], input_v.at[c])
    for c in range(SETS):
        tile = pl.ds(pl.multiple_of((4 * c + me // 4) * LANES, LANES), LANES)
        load(decay_hbm.at[:, tile], param_v.at[c, 0])
        load(freq_hbm.at[:, tile], param_v.at[c, 1])
        load(in_hbm.at[:, :, tile], param_v.at[c, pl.ds(2, 2)])
        load(out_hbm.at[:, :, tile], param_v.at[c, pl.ds(4, 2)])
        load(skip_hbm.at[:, tile], skip_v.at[c])

    barrier = pltpu.get_barrier_semaphore()

    def greet(k, _):
        pl.semaphore_signal(
            barrier, inc=1, device_id={"seq": lax.rem(me + k, SEQ)}, device_id_type=MESH
        )
        return 0

    lax.fori_loop(1, SEQ, greet, 0)
    for k in range(1, DP):
        pl.semaphore_signal(
            barrier, inc=1, device_id={"dp": lax.rem(row + k, DP)}, device_id_type=MESH
        )

    def copy_a(c, there, slot):
        return pltpu.make_async_remote_copy(
            src_ref=send_a.at[c, there],
            dst_ref=recv_a.at[c, slot],
            send_sem=a_send.at[c, there],
            recv_sem=a_recv.at[c, slot],
            device_id={"seq": there},
            device_id_type=MESH,
        )

    def pack(c):
        loads[2 * c].wait()
        loads[2 * c + 1].wait()
        for t in range(4):
            cols = slice(t * LANES, (t + 1) * LANES)
            for k, source in enumerate((grad_v, input_v)):
                tiles = [
                    source[c, q * QUARTER : (q + 1) * QUARTER, cols].astype(F32) for q in range(4)
                ]
                for g, tile in enumerate(swap_blocks(tiles)):
                    send_a[c, 4 * t + g, k * QUARTER : (k + 1) * QUARTER, :] = tile.astype(BF16)

    def launch(c):
        def one(k, _):
            copy_a(c, lax.rem(me + k, SEQ), me).start()
            return 0

        lax.fori_loop(1, SEQ, one, 0)
        recv_a[c, me] = send_a[c, me]

    pack(0)
    pl.semaphore_wait(barrier, SEQ - 1 + DP - 1)
    launch(0)
    pack(1)
    launch(1)

    for copy in loads[2 * SETS :]:
        copy.wait()

    def own(tile, rows):
        acc = pltpu.roll(tile[:rows], lax.rem(4 - own_block, 4) * GROUP, 1)
        for q in range(1, 4):
            part = tile[:rows] if rows == 1 else tile[q * rows : (q + 1) * rows]
            turned = pltpu.roll(part, lax.rem(4 + q - own_block, 4) * GROUP, 1)
            acc = jnp.where(block == q, turned, acc)
        return acc

    for c in range(SETS):
        decay, freq, b_re, b_im, c_re, c_im = [own(param_v[c, k], ROWS) for k in range(6)]
        size = jnp.exp(-(decay / (SEQ * LEN)))
        coef[c, 0, 0] = size * jnp.cos(freq)
        coef[c, 0, 1] = -(size * jnp.sin(freq))
        coef[c, 1] = jnp.zeros((2, ROWS, LANES), F32)
        proj[c, 0] = b_re * c_re + b_im * c_im
        proj[c, 1] = b_im * c_re - b_re * c_im
        proj[c, 2] = c_re
        proj[c, 3] = c_im
        skips[c] = own(skip_v[c], 1)

    first = I32(0)
    slot = lax.broadcasted_iota(I32, (64, LEN), 0)
    place = lax.broadcasted_iota(I32, (64, LEN), 1)
    for j in range(DP):
        length = pieces[0, 0, j]
        chosen = (place - slot == first) & (slot < length)
        pick[j * 64 : (j + 1) * 64, :] = jnp.where(chosen, 1.0, 0.0).astype(BF16)
        first = first + length

    starts = [docs[0, 0]]
    for k in range(1, 3):
        starts.append(starts[-1] + docs[0, k])

    def copy_d(c, there, slot):
        return pltpu.make_async_remote_copy(
            src_ref=send_d.at[c, there],
            dst_ref=recv_d.at[c, slot],
            send_sem=d_send.at[c, there],
            recv_sem=d_recv.at[c, slot],
            device_id={"seq": there},
            device_id_type=MESH,
        )

    def scan_segment(c, t):
        @pl.when(t != me)
        def _():
            copy_a(c, t, t).wait_recv()

        for k, dest in enumerate((gd, ud)):
            tile = recv_a[c, t, k * QUARTER : (k + 1) * QUARTER, :].astype(F32)
            for q, spread in enumerate(spread_blocks(tile)):
                dest[q * QUARTER : (q + 1) * QUARTER, :] = spread

        def positions(b, carry):
            x, y, sx, sy = carry
            base = pl.multiple_of(LEN - (b + 1) * UNROLL, UNROLL)
            whole = t * LEN + base
            for i in range(UNROLL - 1, -1, -1):
                after = whole + (i + 1)
                cut = (after == starts[0]) | (after == starts[1]) | (after == starts[2])
                cut = cut.astype(I32)
                a_re = coef[c, cut, 0]
                a_im = coef[c, cut, 1]
                g = gd[pl.ds(base + i, 1), :]
                u = ud[pl.ds(base + i, 1), :]
                x, y = a_re * x + (g - a_im * y), a_re * y + a_im * x
                sx = sx + u * x
                sy = sy + u * y
                d = proj[c, 0] * x + proj[c, 1] * y
                partial[pl.ds(pl.multiple_of((base + i) * 8, 8), 8), :] = d[:8] + d[8:]
            return x, y, sx, sy

        carry = (state[0], state[1], total[0], total[1])
        carry = lax.fori_loop(0, LEN // UNROLL, positions, carry)
        state[0], state[1], total[0], total[1] = carry

        message = jnp.zeros((QUARTER, LANES), F32)
        for q in range(4):
            tiles = []
            for p in range(QUARTER // 8):
                at = (q * QUARTER + p * 8) * 8
                terms = [partial[pl.ds(at + k, 8, stride=8), :] for k in range(8)]
                while len(terms) > 1:
                    terms = [terms[k] + terms[k + 1] for k in range(0, len(terms), 2)]
                tiles.append(terms[0])
            part = jnp.concatenate(tiles, axis=0)
            part = part + turn(part, 2)
            part = part + turn(part, 1)
            part = part + skips[c] * gd[q * QUARTER : (q + 1) * QUARTER, :]
            message = jnp.where(block == q, part, message)
        message = message.astype(BF16)

        @pl.when(t != me)
        def _():
            send_d[c, t] = message
            copy_d(c, t, me).start()

        @pl.when(t == me)
        def _():
            recv_d[c, me] = message

    def copy_y(c, there, slot):
        cols = pl.ds(pl.multiple_of(c * WIDE, WIDE), WIDE)
        return pltpu.make_async_remote_copy(
            src_ref=send_y.at[c, there],
            dst_ref=ret_ref.at[slot, :, cols],
            send_sem=y_send.at[c, there],
            recv_sem=y_recv.at[c, slot],
            device_id={"dp": there},
            device_id_type=MESH,
        )

    def deliver(c):
        def arrived(k, _):
            other = lax.rem(me + k, SEQ)
            copy_d(c, other, other).wait_recv()
            return 0

        lax.fori_loop(1, SEQ, arrived, 0)
        for t in range(4):
            tiles = [recv_d[c, 4 * t + g].astype(F32) for g in range(4)]
            for q, tile in enumerate(swap_blocks(tiles)):
                rows_d[q * QUARTER : (q + 1) * QUARTER, t * LANES : (t + 1) * LANES] = tile.astype(
                    BF16
                )
        for j in range(DP):
            sent = jnp.dot(
                pick[j * 64 : (j + 1) * 64, :], rows_d[...], preferred_element_type=F32
            ).astype(BF16)
            send_y[c, j] = sent
        for k in range(1, DP):
            copy_y(c, lax.rem(row + k, DP), row).start()
        cols = pl.ds(pl.multiple_of(c * WIDE, WIDE), WIDE)
        ret_ref[row, :, cols] = send_y[c, row]

    def copy_p(c, there, slot):
        return pltpu.make_async_remote_copy(
            src_ref=g_dp.at[c, row],
            dst_ref=g_dp.at[c, slot],
            send_sem=p_send.at[c, there],
            recv_sem=p_recv.at[c, slot],
            device_id={"dp": there},
            device_id_type=MESH,
        )

    def copy_s(c, there, slot):
        return pltpu.make_async_remote_copy(
            src_ref=g_seq.at[c, core, chip],
            dst_ref=g_seq.at[c, core, slot],
            send_sem=s_send.at[c, there],
            recv_sem=s_recv.at[c, slot],
            device_id={"seq": there * 2 + core},
            device_id_type=MESH,
        )

    def copy_c(c, half):
        return pltpu.make_async_remote_copy(
            src_ref=g_seq.at[c, half],
            dst_ref=g_seq.at[c, half],
            send_sem=c_send.at[c],
            recv_sem=c_recv.at[c],
            device_id={"seq": chip * 2 + (1 - core)},
            device_id_type=MESH,
        )

    def sum_own(c):
        sx, sy = total[0], total[1]
        c_re, c_im = proj[c, 2], proj[c, 3]
        g_dp[c, row, 0] = c_re * sx - c_im * sy
        g_dp[c, row, 1] = c_re * sy + c_im * sx
        for k in range(1, DP):
            copy_p(c, lax.rem(row + k, DP), row).start()

    def sum_rows(c):
        for k in range(1, DP):
            other = lax.rem(row + k, DP)
            copy_p(c, other, other).wait_recv()
        scale = math.sqrt(MODES / (DP * SEQ * LEN))
        g_seq[c, core, chip] = ((g_dp[c, 0] + g_dp[c, 1]) + (g_dp[c, 2] + g_dp[c, 3])) * scale
        for k in range(1, SEQ // 2):
            copy_s(c, lax.rem(chip + k, SEQ // 2), chip).start()

    def to_sibling(c):
        for k in range(1, SEQ // 2):
            other = lax.rem(chip + k, SEQ // 2)
            copy_s(c, other, other).wait_recv()
        copy_c(c, core).start()

    def write_sums(c):
        copy_c(c, 1 - core).wait_recv()
        for t in range(4):
            for k in range(2):
                tiles = [g_seq[c, g % 2, (4 * t + g) // 2, k] for g in range(4)]
                for q, tile in enumerate(swap_blocks(tiles)):
                    at = c * WIDE + t * LANES
                    gb_ref[k, q * ROWS : (q + 1) * ROWS, at : at + LANES] = tile

    def step(n, _):
        c = n // SEQ
        t = SEQ - 1 - lax.rem(n, SEQ)

        @pl.when(n == SEQ)
        def _():
            sum_own(0)

        @pl.when(n == SEQ + 4)
        def _():
            sum_rows(0)

        @pl.when(n == SEQ + 9)
        def _():
            to_sibling(0)

        @pl.when(n == SEQ + 12)
        def _():
            write_sums(0)

        @pl.when(t == SEQ - 1)
        def _():
            state[...] = jnp.zeros_like(state)
            total[...] = jnp.zeros_like(total)

        scan_segment(c, t)
        late = n - LAG - (SEQ - 1 - me)

        @pl.when((late == 0) | (late == SEQ))
        def _():
            deliver(late // SEQ)

        return 0

    lax.fori_loop(0, SETS * SEQ, step, 0)
    sum_own(1)

    @pl.when(me < LAG)
    def _():
        deliver(1)

    sum_rows(1)
    to_sibling(1)
    write_sums(1)

    for c in range(SETS):
        for k in range(1, DP):
            other = lax.rem(row + k, DP)
            copy_y(c, other, other).wait_recv()
            copy_y(c, other, row).wait_send()
            copy_p(c, other, row).wait_send()
        for k in range(1, SEQ // 2):
            copy_s(c, lax.rem(chip + k, SEQ // 2), chip).wait_send()
        copy_c(c, core).wait_send()

        def left(k, _):
            other = lax.rem(me + k, SEQ)
            copy_a(c, other, me).wait_send()
            copy_d(c, other, me).wait_send()
            return 0

        lax.fori_loop(1, SEQ, left, 0)


def shards(
    grad_out,
    inputs,
    decay_rate,
    frequency,
    in_proj,
    out_proj,
    skip_gain,
    doc_lengths,
    piece_lengths,
):
    anywhere = pl.BlockSpec(memory_space=pl.ANY)
    scalars = pl.BlockSpec(memory_space=pltpu.SMEM)
    vmem = pl.BlockSpec(memory_space=pltpu.VMEM)
    dma = pltpu.SemaphoreType.DMA
    returned, grad_b = pl.pallas_call(
        kernel,
        out_shape=(
            jax.ShapeDtypeStruct((DP, 64, SETS * WIDE), BF16),
            jax.ShapeDtypeStruct((2, MODES, SETS * WIDE), F32),
        ),
        in_specs=[anywhere] * 7 + [scalars] * 2,
        out_specs=(vmem, vmem),
        scratch_shapes=[
            pltpu.VMEM((SETS, LEN, WIDE), BF16),
            pltpu.VMEM((SETS, LEN, WIDE), BF16),
            pltpu.VMEM((SETS, 6, MODES, LANES), F32),
            pltpu.VMEM((SETS, 1, LANES), F32),
            pltpu.VMEM((SETS, SEQ, 2 * QUARTER, LANES), BF16),
            pltpu.VMEM((SETS, SEQ, 2 * QUARTER, LANES), BF16),
            pltpu.VMEM((SETS, 2, 2, ROWS, LANES), F32),
            pltpu.VMEM((SETS, 4, ROWS, LANES), F32),
            pltpu.VMEM((SETS, 1, LANES), F32),
            pltpu.VMEM((2, ROWS, LANES), F32),
            pltpu.VMEM((2, ROWS, LANES), F32),
            pltpu.VMEM((LEN, LANES), F32),
            pltpu.VMEM((LEN, LANES), F32),
            pltpu.VMEM((LEN * 8, LANES), F32),
            pltpu.VMEM((SETS, SEQ, QUARTER, LANES), BF16),
            pltpu.VMEM((SETS, SEQ, QUARTER, LANES), BF16),
            pltpu.VMEM((LEN, WIDE), BF16),
            pltpu.VMEM((DP * 64, LEN), BF16),
            pltpu.VMEM((SETS, DP, 64, WIDE), BF16),
            pltpu.VMEM((SETS, DP, 2, ROWS, LANES), F32),
            pltpu.VMEM((SETS, 2, SEQ // 2, 2, ROWS, LANES), F32),
            dma((7 * SETS,)),
            dma((SETS, SEQ)),
            dma((SETS, SEQ)),
            dma((SETS, SEQ)),
            dma((SETS, SEQ)),
            dma((SETS, DP)),
            dma((SETS, DP)),
            dma((SETS, DP)),
            dma((SETS, DP)),
            dma((SETS, SEQ // 2)),
            dma((SETS, SEQ // 2)),
            dma((SETS,)),
            dma((SETS,)),
        ],
        compiler_params=pltpu.CompilerParams(
            collective_id=0, has_side_effects=True, vmem_limit_bytes=32 << 20
        ),
        cost_estimate=pl.CostEstimate(
            flops=15 * 128 * 64 * 1024, bytes_accessed=4 << 20, transcendentals=0
        ),
        name="scan_rows",
    )(
        grad_out,
        inputs,
        decay_rate,
        frequency,
        in_proj,
        out_proj,
        skip_gain[None],
        doc_lengths,
        piece_lengths,
    )
    return returned[None, None], grad_b


def solution(mesh):
    return jax.shard_map(
        shards,
        mesh=mesh,
        in_specs=(
            P("dp", "seq", "ch"),
            P("dp", "seq", "ch"),
            P(None, "ch"),
            P(None, "ch"),
            P(None, None, "ch"),
            P(None, None, "ch"),
            P("ch"),
            P("dp", None),
            P("dp", "seq", None),
        ),
        out_specs=(P("seq", "dp", None, None, "ch"), P(None, None, "ch")),
        check_vma=False,
    )
```

time: 896 us -> 93.6 us (0.10)
  waiting for transfers between devices: 300 us -> 0 us
  other arithmetic: 248 us -> 0 us
  local copies, waits for them, and re-layouts: 150 us -> 8.81 us
  matrix products: 102 us -> 0 us
  Pallas kernels: 0 us -> 83.8 us
  starting transfers between devices: 64.2 us -> 0 us
  between operations: 14.4 us -> 0.67 us
  loops' own time: 11.5 us -> 0 us
    psum x1 -> x0, waiting for transfers between devices: 198 us -> none  [shards(): reduced = lax.psum((grad_re, grad_im), ('seq', 'dp'))]
    mul x35 -> x0, other arithmetic: 157 us -> none  [the longest x16 138 us: mode_powers(): decay_pow * jnp.cos(phases)]
    ppermute x30 -> x0, waiting for transfers between devices: 102 us -> none  [from_behind(): lax.ppermute(value, axis, [(source, source + steps) for source in range(i...]
    dot_general x24 -> x0, matrix products: 102 us -> none  [the longest x8 45.7 us: local_group(): jnp.einsum('kmc,vkc->vmc', powers, stacked, precision=exact_precision)]
    pallas_call x0 -> x1, Pallas kernels: none -> 83.8 us  [shards(): pl.pallas_call(kernel, out_shape=(jax.ShapeDtypeStruct((DP, 64, SETS * WI...]
    ppermute x30 -> x0, starting transfers between devices: 60.7 us -> none  [from_behind(): lax.ppermute(value, axis, [(source, source + steps) for source in range(i...]
    dynamic_slice x72 -> x0, local copies, waits for them, and re-layouts: 42.7 us -> none  [the longest x48 23.2 us: pick_group(): lax.dynamic_slice_in_dim(source, group_id * group_width, group_width, sou...]
    dot_general x16 -> x0, other arithmetic: 36.7 us -> none  [the longest x8 20.4 us: local_group(): jnp.einsum('jtkc,jtc->kc', shifted, input_group, precision=exact_precision)]
  transfers between devices with their start and end apart: 32 -> 0, of which waited for: 31 -> 0; matrix products, arithmetic and copies ran while one was open for 1% -> 0% of each run, Pallas kernels for 0% -> 0%
where the time goes in v1:
time: 93.6 us; the launch traced here: 93.3 us
  Pallas kernels  83.8 us (90%)
  local copies, waits for them, and re-layouts  8.81 us (9%)
    pallas_call x1, Pallas kernels, shards(): pl.pallas_call(kernel, out_shape=(jax.ShapeDtypeStruct((DP, 64, SETS * WI...  83.8 us
    unnamed x20, local copies, waits for them, and re-layouts  8.81 us

profile of v1, /device:TPU:1, one launch (start us, length us, event | category | flops | bytes accessed | tf_op | source)
XLA Modules:
  0.0 93.3 jit_solution(14113034461017360829)
XLA Ops:
  0.6 0.0 copy-start.8
  0.6 0.0 copy-start.7
  0.7 0.6 copy-done.8
  1.3 0.0 copy-done.7
  1.3 0.0 copy-start
  1.3 1.0 %copy-done = f32[2,64,1024]{2,1,0:T(8,128)S(1)} copy-done((f32[2,64,1024]{2,1,0:T(8,128)S(1)}, f32[2,64,1024]{2,1,0:T(8,128)}, u32[]{:S(2)}) %copy-start) | copy-done | bytes 524312
  2.3 0.0 copy-start.1
  2.3 1.0 %copy-done.1 = f32[2,64,1024]{2,1,0:T(8,128)S(1)} copy-done((f32[2,64,1024]{2,1,0:T(8,128)S(1)}, f32[2,64,1024]{2,1,0:T(8,128)}, u32[]{:S(2)}) %copy-start.1) | copy-done | bytes 524312
  3.4 0.0 copy-start.2
  3.4 0.9 %copy-done.2 = bf16[1,128,1024]{2,1,0:T(8,128)(2,1)S(1)} copy-done((bf16[1,128,1024]{2,1,0:T(8,128)(2,1)S(1)}, bf16[1,128,1024]{2,1,0:T(8,128)(2,1)}, u32[]{:S(2)}) %copy-start.2) | copy-done | bytes 262168
  4.3 0.0 copy-start.3
  4.3 0.9 %copy-done.3 = bf16[1,128,1024]{2,1,0:T(8,128)(2,1)S(1)} copy-done((bf16[1,128,1024]{2,1,0:T(8,128)(2,1)S(1)}, bf16[1,128,1024]{2,1,0:T(8,128)(2,1)}, u32[]{:S(2)}) %copy-start.3) | copy-done | bytes 262168
  5.3 0.0 copy-start.4
  5.3 0.9 %copy-done.4 = f32[64,1024]{1,0:T(8,128)S(1)} copy-done((f32[64,1024]{1,0:T(8,128)S(1)}, f32[64,1024]{1,0:T(8,128)}, u32[]{:S(2)}) %copy-start.4) | copy-done | bytes 262168
  6.2 0.0 copy-start.5
  6.2 0.9 %copy-done.5 = f32[64,1024]{1,0:T(8,128)S(1)} copy-done((f32[64,1024]{1,0:T(8,128)S(1)}, f32[64,1024]{1,0:T(8,128)}, u32[]{:S(2)}) %copy-start.5) | copy-done | bytes 262168
  7.2 0.0 copy-start.6
  7.2 0.7 copy-done.6
  7.9 83.8 %scan_rows.1 = (bf16[4,64,1024]{2,1,0:T(8,128)(2,1)S(1)}, f32[2,64,1024]{2,1,0:T(8,128)S(1)}) custom-call(bf16[1,128,1024]{2,1,0:T(8,128)(2,1)S(1)} %copy-done.2, bf16[1,128,1024]{2,1,0:T(8,128)(2,1)S(1)} %copy-done.3, f32[64,1024]{1,0:T(8,128)S(1)} %copy-done.4, f32[64,1024]{1,0:T(8,128)S(1)} %copy-done.5, f32[2,64,1024]{2,1,0:T(8,128)S(1)} %copy-done, ...), custom_call_target="tpu_custom_call" | custom-call | flops 125829120 | bytes 4194304 | tf_op jit(solution)/shard_map/scan_rows/pallas_call | solution.py:463
  91.7 0.8 copy.13
  92.5 0.8 copy.14
Async XLA Ops:
  0.6 0.7 copy-start.8
  0.6 0.7 copy-start.7
  1.3 1.0 %copy-start = (f32[2,64,1024]{2,1,0:T(8,128)S(1)}, f32[2,64,1024]{2,1,0:T(8,128)}, u32[]{:S(2)}) copy-start(f32[2,64,1024]{2,1,0:T(8,128)} %in_hbm.1) | copy-start | bytes 1572868
  2.3 1.0 %copy-start.1 = (f32[2,64,1024]{2,1,0:T(8,128)S(1)}, f32[2,64,1024]{2,1,0:T(8,128)}, u32[]{:S(2)}) copy-start(f32[2,64,1024]{2,1,0:T(8,128)} %out_hbm.1) | copy-start | bytes 1572868
  3.4 0.9 %copy-start.2 = (bf16[1,128,1024]{2,1,0:T(8,128)(2,1)S(1)}, bf16[1,128,1024]{2,1,0:T(8,128)(2,1)}, u32[]{:S(2)}) copy-start(bf16[1,128,1024]{2,1,0:T(8,128)(2,1)} %grad_hbm.1) | copy-start | bytes 786436
  4.3 0.9 %copy-start.3 = (bf16[1,128,1024]{2,1,0:T(8,128)(2,1)S(1)}, bf16[1,128,1024]{2,1,0:T(8,128)(2,1)}, u32[]{:S(2)}) copy-start(bf16[1,128,1024]{2,1,0:T(8,128)(2,1)} %input_hbm.1) | copy-start | bytes 786436
  5.3 0.9 %copy-start.4 = (f32[64,1024]{1,0:T(8,128)S(1)}, f32[64,1024]{1,0:T(8,128)}, u32[]{:S(2)}) copy-start(f32[64,1024]{1,0:T(8,128)} %decay_hbm.1) | copy-start | bytes 786436
  6.2 0.9 %copy-start.5 = (f32[64,1024]{1,0:T(8,128)S(1)}, f32[64,1024]{1,0:T(8,128)}, u32[]{:S(2)}) copy-start(f32[64,1024]{1,0:T(8,128)} %freq_hbm.1) | copy-start | bytes 786436
  7.2 0.7 copy-start.6

commit v2 on v1

--- a/solution.py
+++ b/solution.py
@@ -22,8 +22,7 @@
 QUARTER = 32
 MODES = 64
 ROWS = 16
-UNROLL = 16
-LAG = 2
+HALF = SEQ // 2
 
 
 def lane_block():
@@ -33,6 +32,41 @@
 def turn(tile, blocks):
     shift = (blocks % 4) * GROUP
     return tile if shift == 0 else pltpu.roll(tile, shift, 1)
+
+
+def interleave(tile):
+    return [
+        jnp.concatenate([tile[32 * r + 8 * b : 32 * r + 8 * b + 8] for r in range(4)], axis=0)
+        for b in range(4)
+    ]
+
+
+def fold_rows(tiles):
+    place = lax.broadcasted_iota(I32, (8, 1), 0)
+    for step in (1, 2, 4):
+        first = (place & step) == 0
+        out = []
+        half = len(tiles) // 2
+        pairs = [(2 * k, 2 * k + 1) for k in range(half)]
+        for one, two in pairs:
+            kept = jnp.where(first, tiles[one], tiles[two])
+            moved = jnp.where(first, tiles[two], tiles[one])
+            out.append(kept + pltpu.roll(moved, 8 - step, 0))
+        tiles = out
+    return tiles[0]
+
+
+def fold_blocks(tiles):
+    block = lane_block()
+    for step in (1, 2):
+        first = (block & step) == 0
+        out = []
+        for one, two in [(2 * k, 2 * k + 1) for k in range(len(tiles) // 2)]:
+            kept = jnp.where(first, tiles[one], tiles[two])
+            moved = jnp.where(first, tiles[two], tiles[one])
+            out.append(kept + turn(moved, -step))
+        tiles = out
+    return tiles[0]
 
 
 def swap_blocks(tiles):
@@ -90,7 +124,7 @@
     pick,
     send_y,
     g_dp,
-    g_seq,
+    g_all,
     load_sem,
     a_send,
     a_recv,
@@ -102,13 +136,9 @@
     p_recv,
     s_send,
     s_recv,
-    c_send,
-    c_recv,
 ):
     me = lax.axis_index("seq")
     row = lax.axis_index("dp")
-    core = lax.rem(me, 2)
-    chip = me // 2
     block = lane_block()
     own_block = lax.rem(me, 4)
 
@@ -161,9 +191,7 @@
         for t in range(4):
             cols = slice(t * LANES, (t + 1) * LANES)
             for k, source in enumerate((grad_v, input_v)):
-                tiles = [
-                    source[c, q * QUARTER : (q + 1) * QUARTER, cols].astype(F32) for q in range(4)
-                ]
+                tiles = interleave(source[c, :, cols].astype(F32))
                 for g, tile in enumerate(swap_blocks(tiles)):
                     send_a[c, 4 * t + g, k * QUARTER : (k + 1) * QUARTER, :] = tile.astype(BF16)
 
@@ -227,6 +255,11 @@
             device_id_type=MESH,
         )
 
+    def send_home(c, t):
+        @pl.when(t != me)
+        def _():
+            copy_d(c, t, me).start()
+
     def scan_segment(c, t):
         @pl.when(t != me)
         def _():
@@ -234,52 +267,38 @@
 
         for k, dest in enumerate((gd, ud)):
             tile = recv_a[c, t, k * QUARTER : (k + 1) * QUARTER, :].astype(F32)
-            for q, spread in enumerate(spread_blocks(tile)):
-                dest[q * QUARTER : (q + 1) * QUARTER, :] = spread
-
-        def positions(b, carry):
-            x, y, sx, sy = carry
-            base = pl.multiple_of(LEN - (b + 1) * UNROLL, UNROLL)
-            whole = t * LEN + base
-            for i in range(UNROLL - 1, -1, -1):
-                after = whole + (i + 1)
-                cut = (after == starts[0]) | (after == starts[1]) | (after == starts[2])
-                cut = cut.astype(I32)
-                a_re = coef[c, cut, 0]
-                a_im = coef[c, cut, 1]
-                g = gd[pl.ds(base + i, 1), :]
-                u = ud[pl.ds(base + i, 1), :]
-                x, y = a_re * x + (g - a_im * y), a_re * y + a_im * x
-                sx = sx + u * x
-                sy = sy + u * y
-                d = proj[c, 0] * x + proj[c, 1] * y
-                partial[pl.ds(pl.multiple_of((base + i) * 8, 8), 8), :] = d[:8] + d[8:]
-            return x, y, sx, sy
-
-        carry = (state[0], state[1], total[0], total[1])
-        carry = lax.fori_loop(0, LEN // UNROLL, positions, carry)
-        state[0], state[1], total[0], total[1] = carry
-
-        message = jnp.zeros((QUARTER, LANES), F32)
-        for q in range(4):
-            tiles = []
-            for p in range(QUARTER // 8):
-                at = (q * QUARTER + p * 8) * 8
-                terms = [partial[pl.ds(at + k, 8, stride=8), :] for k in range(8)]
-                while len(terms) > 1:
-                    terms = [terms[k] + terms[k + 1] for k in range(0, len(terms), 2)]
-                tiles.append(terms[0])
-            part = jnp.concatenate(tiles, axis=0)
-            part = part + turn(part, 2)
-            part = part + turn(part, 1)
-            part = part + skips[c] * gd[q * QUARTER : (q + 1) * QUARTER, :]
-            message = jnp.where(block == q, part, message)
+            for b, spread in enumerate(spread_blocks(tile)):
+                for r in range(4):
+                    at = 32 * r + 8 * b
+                    dest[at : at + 8, :] = spread[8 * r : 8 * r + 8]
+
+        x, y, sx, sy = state[0], state[1], total[0], total[1]
+        sums = []
+        for i in range(LEN - 1, -1, -1):
+            after = t * LEN + (i + 1)
+            cut = (after == starts[0]) | (after == starts[1]) | (after == starts[2])
+            cut = cut.astype(I32)
+            a_re = coef[c, cut, 0]
+            a_im = coef[c, cut, 1]
+            g = gd[i : i + 1, :]
+            u = ud[i : i + 1, :]
+            x, y = a_re * x + (g - a_im * y), a_re * y + a_im * x
+            sx = sx + u * x
+            sy = sy + u * y
+            d = proj[c, 0] * x + proj[c, 1] * y
+            sums.insert(0, d[:8] + d[8:])
+            if i % 8 == 0:
+                partial[i : i + 8, :] = fold_rows(sums)
+                sums = []
+        state[0], state[1], total[0], total[1] = x, y, sx, sy
+
+        message = fold_blocks(interleave(partial[...]))
+        message = message + skips[c] * recv_a[c, t, :QUARTER, :].astype(F32)
         message = message.astype(BF16)
 
         @pl.when(t != me)
         def _():
             send_d[c, t] = message
-            copy_d(c, t, me).start()
 
         @pl.when(t == me)
         def _():
@@ -305,10 +324,10 @@
         lax.fori_loop(1, SEQ, arrived, 0)
         for t in range(4):
             tiles = [recv_d[c, 4 * t + g].astype(F32) for g in range(4)]
-            for q, tile in enumerate(swap_blocks(tiles)):
-                rows_d[q * QUARTER : (q + 1) * QUARTER, t * LANES : (t + 1) * LANES] = tile.astype(
-                    BF16
-                )
+            tiles = swap_blocks(tiles)
+            whole = [tiles[b][8 * r : 8 * r + 8] for r in range(4) for b in range(4)]
+            whole = jnp.concatenate(whole, axis=0)
+            rows_d[:, t * LANES : (t + 1) * LANES] = whole.astype(BF16)
         for j in range(DP):
             sent = jnp.dot(
                 pick[j * 64 : (j + 1) * 64, :], rows_d[...], preferred_element_type=F32
@@ -331,21 +350,11 @@
 
     def copy_s(c, there, slot):
         return pltpu.make_async_remote_copy(
-            src_ref=g_seq.at[c, core, chip],
-            dst_ref=g_seq.at[c, core, slot],
+            src_ref=g_all.at[c, me],
+            dst_ref=g_all.at[c, slot],
             send_sem=s_send.at[c, there],
             recv_sem=s_recv.at[c, slot],
-            device_id={"seq": there * 2 + core},
-            device_id_type=MESH,
-        )
-
-    def copy_c(c, half):
-        return pltpu.make_async_remote_copy(
-            src_ref=g_seq.at[c, half],
-            dst_ref=g_seq.at[c, half],
-            send_sem=c_send.at[c],
-            recv_sem=c_recv.at[c],
-            device_id={"seq": chip * 2 + (1 - core)},
+            device_id={"seq": there},
             device_id_type=MESH,
         )
 
@@ -362,24 +371,27 @@
             other = lax.rem(row + k, DP)
             copy_p(c, other, other).wait_recv()
         scale = math.sqrt(MODES / (DP * SEQ * LEN))
-        g_seq[c, core, chip] = ((g_dp[c, 0] + g_dp[c, 1]) + (g_dp[c, 2] + g_dp[c, 3])) * scale
-        for k in range(1, SEQ // 2):
-            copy_s(c, lax.rem(chip + k, SEQ // 2), chip).start()
-
-    def to_sibling(c):
-        for k in range(1, SEQ // 2):
-            other = lax.rem(chip + k, SEQ // 2)
+        g_all[c, me] = ((g_dp[c, 0] + g_dp[c, 1]) + (g_dp[c, 2] + g_dp[c, 3])) * scale
+
+        def one(k, _):
+            copy_s(c, lax.rem(me + k, SEQ), me).start()
+            return 0
+
+        lax.fori_loop(1, SEQ, one, 0)
+
+    def write_sums(c):
+        def one(k, _):
+            other = lax.rem(me + k, SEQ)
             copy_s(c, other, other).wait_recv()
-        copy_c(c, core).start()
-
-    def write_sums(c):
-        copy_c(c, 1 - core).wait_recv()
+            return 0
+
+        lax.fori_loop(1, SEQ, one, 0)
         for t in range(4):
+            cols = slice(c * WIDE + t * LANES, c * WIDE + (t + 1) * LANES)
             for k in range(2):
-                tiles = [g_seq[c, g % 2, (4 * t + g) // 2, k] for g in range(4)]
+                tiles = [g_all[c, 4 * t + g, k] for g in range(4)]
                 for q, tile in enumerate(swap_blocks(tiles)):
-                    at = c * WIDE + t * LANES
-                    gb_ref[k, q * ROWS : (q + 1) * ROWS, at : at + LANES] = tile
+                    gb_ref[k, q * ROWS : (q + 1) * ROWS, cols] = tile
 
     def step(n, _):
         c = n // SEQ
@@ -393,13 +405,12 @@
         def _():
             sum_rows(0)
 
-        @pl.when(n == SEQ + 9)
-        def _():
-            to_sibling(0)
-
-        @pl.when(n == SEQ + 12)
-        def _():
-            write_sums(0)
+        last = n - SEQ
+
+        @pl.when((last >= 0) & (last < HALF))
+        def _():
+            send_home(0, lax.rem(me + 2 * last + 1, SEQ))
+            send_home(0, lax.rem(me + 2 * last + 2, SEQ))
 
         @pl.when(t == SEQ - 1)
         def _():
@@ -407,23 +418,45 @@
             total[...] = jnp.zeros_like(total)
 
         scan_segment(c, t)
-        late = n - LAG - (SEQ - 1 - me)
-
-        @pl.when((late == 0) | (late == SEQ))
-        def _():
-            deliver(late // SEQ)
+
+        @pl.when((last >= HALF - 1) & (last < HALF + 3))
+        def _():
+            for k in range(2):
+                send_home(1, HALF + lax.rem(me + 2 * (last + 1) + k, HALF))
+
+        @pl.when((last >= HALF + 3) & (last < HALF + 5))
+        def _():
+            for k in range(2):
+                send_home(1, HALF // 2 + lax.rem(me + 2 * (last + 1) + k, HALF // 2))
+
+        @pl.when(last == HALF + 5)
+        def _():
+            for k in range(2):
+                send_home(1, 2 + lax.rem(me + k, 2))
+
+        @pl.when(last >= HALF + 6)
+        def _():
+            send_home(1, t)
+
+        @pl.when(last == SEQ - 3)
+        def _():
+            deliver(0)
+
+        @pl.when((last == SEQ - 2) & (me >= HALF))
+        def _():
+            deliver(1)
 
         return 0
 
     lax.fori_loop(0, SETS * SEQ, step, 0)
     sum_own(1)
-
-    @pl.when(me < LAG)
+    write_sums(0)
+    sum_rows(1)
+
+    @pl.when(me < HALF)
     def _():
         deliver(1)
 
-    sum_rows(1)
-    to_sibling(1)
     write_sums(1)
 
     for c in range(SETS):
@@ -432,14 +465,12 @@
             copy_y(c, other, other).wait_recv()
             copy_y(c, other, row).wait_send()
             copy_p(c, other, row).wait_send()
-        for k in range(1, SEQ // 2):
-            copy_s(c, lax.rem(chip + k, SEQ // 2), chip).wait_send()
-        copy_c(c, core).wait_send()
 
         def left(k, _):
             other = lax.rem(me + k, SEQ)
             copy_a(c, other, me).wait_send()
             copy_d(c, other, me).wait_send()
+            copy_s(c, other, me).wait_send()
             return 0
 
         lax.fori_loop(1, SEQ, left, 0)
@@ -482,14 +513,14 @@
             pltpu.VMEM((2, ROWS, LANES), F32),
             pltpu.VMEM((LEN, LANES), F32),
             pltpu.VMEM((LEN, LANES), F32),
-            pltpu.VMEM((LEN * 8, LANES), F32),
+            pltpu.VMEM((LEN, LANES), F32),
             pltpu.VMEM((SETS, SEQ, QUARTER, LANES), BF16),
             pltpu.VMEM((SETS, SEQ, QUARTER, LANES), BF16),
             pltpu.VMEM((LEN, WIDE), BF16),
             pltpu.VMEM((DP * 64, LEN), BF16),
             pltpu.VMEM((SETS, DP, 64, WIDE), BF16),
             pltpu.VMEM((SETS, DP, 2, ROWS, LANES), F32),
-            pltpu.VMEM((SETS, 2, SEQ // 2, 2, ROWS, LANES), F32),
+            pltpu.VMEM((SETS, SEQ, 2, ROWS, LANES), F32),
             dma((7 * SETS,)),
             dma((SETS, SEQ)),
             dma((SETS, SEQ)),
@@ -499,13 +530,11 @@
             dma((SETS, DP)),
             dma((SETS, DP)),
             dma((SETS, DP)),
-            dma((SETS, SEQ // 2)),
-            dma((SETS, SEQ // 2)),
-            dma((SETS,)),
-            dma((SETS,)),
+            dma((SETS, SEQ)),
+            dma((SETS, SEQ)),
         ],
         compiler_params=pltpu.CompilerParams(
-            collective_id=0, has_side_effects=True, vmem_limit_bytes=32 << 20
+            collective_id=0, has_side_effects=True, vmem_limit_bytes=62 << 20
         ),
         cost_estimate=pl.CostEstimate(
             flops=15 * 128 * 64 * 1024, bytes_accessed=4 << 20, transcendentals=0

time: 93.6 us -> 67.1 us (0.72)
  Pallas kernels: 83.8 us -> 63.6 us
  local copies, waits for them, and re-layouts: 8.81 us -> 2.72 us
    pallas_call x1, Pallas kernels: 83.8 us -> 63.6 us  [shards(): pl.pallas_call(kernel, out_shape=(jax.ShapeDtypeStruct((DP, 64, SETS * WI...]
    unnamed x20 -> x4, local copies, waits for them, and re-layouts: 8.81 us -> 2.72 us
where the time goes in v2:
time: 67.1 us; the launch traced here: 67 us
  Pallas kernels  63.6 us (95%)
  local copies, waits for them, and re-layouts  2.72 us (4%)
    pallas_call x1, Pallas kernels, shards(): pl.pallas_call(kernel, out_shape=(jax.ShapeDtypeStruct((DP, 64, SETS * WI...  63.6 us
    unnamed x4, local copies, waits for them, and re-layouts  2.72 us

profile of v2, /device:TPU:1, one launch (start us, length us, event | category | flops | bytes accessed | tf_op | source)
XLA Modules:
  0.0 67.0 jit_solution(7530015493252925785)
XLA Ops:
  0.6 63.6 %scan_rows.1 = (bf16[4,64,1024]{2,1,0:T(8,128)(2,1)}, f32[2,64,1024]{2,1,0:T(8,128)}) custom-call(bf16[1,128,1024]{2,1,0:T(8,128)(2,1)} %grad_hbm.1, bf16[1,128,1024]{2,1,0:T(8,128)(2,1)} %input_hbm.1, f32[64,1024]{1,0:T(8,128)} %decay_hbm.1, f32[64,1024]{1,0:T(8,128)} %freq_hbm.1, f32[2,64,1024]{2,1,0:T(8,128)} %in_hbm.1, f32[2,64,1024]{2,1,0:T(8,128)} %out_hbm.1, ...), custom_call_target="tpu_custom_call" | custom-call | flops 125829120 | bytes 4194304 | tf_op jit(solution)/shard_map/scan_rows/pallas_call | solution.py:494
  64.2 0.0 copy-start
  64.2 1.9 %copy.13 = bf16[1,1,4,64,1024]{4,3,2,1,0:T(8,128)(2,1)} copy(bf16[1,1,4,64,1024]{4,3,2,1,0:T(8,128)(2,1)} %bitcast.2) | data formatting | bytes 1048576
  66.2 0.0 copy-done
  66.2 0.8 %copy.14 = f32[2,64,1024]{2,1,0:T(8,128)} copy(f32[2,64,1024]{2,1,0:T(8,128)S(1)} %copy-done) | data formatting | bytes 1048576
Async XLA Ops:
  64.2 1.9 %copy-start = (f32[2,64,1024]{2,1,0:T(8,128)S(1)}, f32[2,64,1024]{2,1,0:T(8,128)}, u32[]{:S(2)}) copy-start(f32[2,64,1024]{2,1,0:T(8,128)} %get-tuple-element.9) | copy-start | bytes 1572868

commit v3 on v2

--- a/solution.py
+++ b/solution.py
@@ -23,6 +23,7 @@
 MODES = 64
 ROWS = 16
 HALF = SEQ // 2
+SECOND = 3
 
 
 def lane_block():
@@ -136,8 +137,12 @@
     p_recv,
     s_send,
     s_recv,
+    c_send,
+    c_recv,
 ):
     me = lax.axis_index("seq")
+    core = lax.rem(me, 2)
+    chip = me // 2
     row = lax.axis_index("dp")
     block = lane_block()
     own_block = lax.rem(me, 4)
@@ -207,7 +212,6 @@
     pl.semaphore_wait(barrier, SEQ - 1 + DP - 1)
     launch(0)
     pack(1)
-    launch(1)
 
     for copy in loads[2 * SETS :]:
         copy.wait()
@@ -350,11 +354,21 @@
 
     def copy_s(c, there, slot):
         return pltpu.make_async_remote_copy(
-            src_ref=g_all.at[c, me],
-            dst_ref=g_all.at[c, slot],
+            src_ref=g_all.at[c, core, chip],
+            dst_ref=g_all.at[c, core, slot],
             send_sem=s_send.at[c, there],
             recv_sem=s_recv.at[c, slot],
-            device_id={"seq": there},
+            device_id={"seq": 2 * there + core},
+            device_id_type=MESH,
+        )
+
+    def copy_c(c, half):
+        return pltpu.make_async_remote_copy(
+            src_ref=g_all.at[c, half],
+            dst_ref=g_all.at[c, half],
+            send_sem=c_send.at[c],
+            recv_sem=c_recv.at[c],
+            device_id={"seq": 2 * chip + 1 - core},
             device_id_type=MESH,
         )
 
@@ -371,25 +385,22 @@
             other = lax.rem(row + k, DP)
             copy_p(c, other, other).wait_recv()
         scale = math.sqrt(MODES / (DP * SEQ * LEN))
-        g_all[c, me] = ((g_dp[c, 0] + g_dp[c, 1]) + (g_dp[c, 2] + g_dp[c, 3])) * scale
-
-        def one(k, _):
-            copy_s(c, lax.rem(me + k, SEQ), me).start()
-            return 0
-
-        lax.fori_loop(1, SEQ, one, 0)
+        g_all[c, core, chip] = ((g_dp[c, 0] + g_dp[c, 1]) + (g_dp[c, 2] + g_dp[c, 3])) * scale
+        for k in range(1, HALF):
+            copy_s(c, lax.rem(chip + k, HALF), chip).start()
+
+    def to_sibling(c):
+        for k in range(1, HALF):
+            other = lax.rem(chip + k, HALF)
+            copy_s(c, other, other).wait_recv()
+        copy_c(c, core).start()
 
     def write_sums(c):
-        def one(k, _):
-            other = lax.rem(me + k, SEQ)
-            copy_s(c, other, other).wait_recv()
-            return 0
-
-        lax.fori_loop(1, SEQ, one, 0)
+        copy_c(c, 1 - core).wait_recv()
         for t in range(4):
             cols = slice(c * WIDE + t * LANES, c * WIDE + (t + 1) * LANES)
             for k in range(2):
-                tiles = [g_all[c, 4 * t + g, k] for g in range(4)]
+                tiles = [g_all[c, g % 2, 2 * t + g // 2, k] for g in range(4)]
                 for q, tile in enumerate(swap_blocks(tiles)):
                     gb_ref[k, q * ROWS : (q + 1) * ROWS, cols] = tile
 
@@ -397,6 +408,10 @@
         c = n // SEQ
         t = SEQ - 1 - lax.rem(n, SEQ)
 
+        @pl.when(n == SECOND)
+        def _():
+            launch(1)
+
         @pl.when(n == SEQ)
         def _():
             sum_own(0)
@@ -450,13 +465,15 @@
 
     lax.fori_loop(0, SETS * SEQ, step, 0)
     sum_own(1)
-    write_sums(0)
+    to_sibling(0)
     sum_rows(1)
 
     @pl.when(me < HALF)
     def _():
         deliver(1)
 
+    to_sibling(1)
+    write_sums(0)
     write_sums(1)
 
     for c in range(SETS):
@@ -465,15 +482,27 @@
             copy_y(c, other, other).wait_recv()
             copy_y(c, other, row).wait_send()
             copy_p(c, other, row).wait_send()
+        for k in range(1, HALF):
+            copy_s(c, lax.rem(chip + k, HALF), chip).wait_send()
+        copy_c(c, core).wait_send()
 
         def left(k, _):
             other = lax.rem(me + k, SEQ)
             copy_a(c, other, me).wait_send()
             copy_d(c, other, me).wait_send()
-            copy_s(c, other, me).wait_send()
             return 0
 
         lax.fori_loop(1, SEQ, left, 0)
+
+
+def place_kernel(ret_in, gb_in, ret_out, gb_out, sem):
+    copies = [
+        pltpu.make_async_copy(ret_in.at[k], ret_out.at[k], sem.at[k]) for k in range(DP)
+    ] + [pltpu.make_async_copy(gb_in.at[k], gb_out.at[k], sem.at[DP + k]) for k in range(2)]
+    for copy in copies:
+        copy.start()
+    for copy in copies:
+        copy.wait()
 
 
 def shards(
@@ -520,7 +549,7 @@
             pltpu.VMEM((DP * 64, LEN), BF16),
             pltpu.VMEM((SETS, DP, 64, WIDE), BF16),
             pltpu.VMEM((SETS, DP, 2, ROWS, LANES), F32),
-            pltpu.VMEM((SETS, SEQ, 2, ROWS, LANES), F32),
+            pltpu.VMEM((SETS, 2, HALF, 2, ROWS, LANES), F32),
             dma((7 * SETS,)),
             dma((SETS, SEQ)),
             dma((SETS, SEQ)),
@@ -530,8 +559,10 @@
             dma((SETS, DP)),
             dma((SETS, DP)),
             dma((SETS, DP)),
-            dma((SETS, SEQ)),
-            dma((SETS, SEQ)),
+            dma((SETS, HALF)),
+            dma((SETS, HALF)),
+            dma((SETS,)),
+            dma((SETS,)),
         ],
         compiler_params=pltpu.CompilerParams(
             collective_id=0, has_side_effects=True, vmem_limit_bytes=62 << 20
@@ -551,6 +582,18 @@
         doc_lengths,
         piece_lengths,
     )
+    returned, grad_b = pl.pallas_call(
+        place_kernel,
+        out_shape=(
+            jax.ShapeDtypeStruct(returned.shape, BF16),
+            jax.ShapeDtypeStruct(grad_b.shape, F32),
+        ),
+        in_specs=[vmem] * 2,
+        out_specs=(anywhere, anywhere),
+        scratch_shapes=[dma((DP + 2,))],
+        compiler_params=pltpu.CompilerParams(vmem_limit_bytes=62 << 20),
+        name="place_results",
+    )(returned, grad_b)
     return returned[None, None], grad_b
 
 

time: 67.1 us -> 64.3 us (0.958)
  local copies, waits for them, and re-layouts: 2.72 us -> 0 us
    unnamed x4 -> x0, local copies, waits for them, and re-layouts: 2.72 us -> none
    pallas_call x1, Pallas kernels: 63.6 us -> 61.3 us  [shards(): pl.pallas_call(kernel, out_shape=(jax.ShapeDtypeStruct((DP, 64, SETS * WI...]
    pallas_call x0 -> x1, Pallas kernels: none -> 2.21 us  [shards(): pl.pallas_call(place_kernel, out_shape=(jax.ShapeDtypeStruct(returned.sha...]
where the time goes in v3:
time: 64.3 us; the launch traced here: 64.2 us
  Pallas kernels  63.6 us (99%)
    pallas_call x1, Pallas kernels, shards(): pl.pallas_call(kernel, out_shape=(jax.ShapeDtypeStruct((DP, 64, SETS * WI...  61.3 us
    pallas_call x1, Pallas kernels, shards(): pl.pallas_call(place_kernel, out_shape=(jax.ShapeDtypeStruct(returned.sha...  2.21 us

profile of v3, /device:TPU:1, one launch (start us, length us, event | category | flops | bytes accessed | tf_op | source)
XLA Modules:
  0.0 64.2 jit_solution(8938569022857709143)
XLA Ops:
  0.6 61.3 %scan_rows.1 = (bf16[4,64,1024]{2,1,0:T(8,128)(2,1)}, f32[2,64,1024]{2,1,0:T(8,128)}) custom-call(bf16[1,128,1024]{2,1,0:T(8,128)(2,1)} %grad_hbm.1, bf16[1,128,1024]{2,1,0:T(8,128)(2,1)} %input_hbm.1, f32[64,1024]{1,0:T(8,128)} %decay_hbm.1, f32[64,1024]{1,0:T(8,128)} %freq_hbm.1, f32[2,64,1024]{2,1,0:T(8,128)} %in_hbm.1, f32[2,64,1024]{2,1,0:T(8,128)} %out_hbm.1, ...), custom_call_target="tpu_custom_call" | custom-call | flops 125829120 | bytes 4194304 | tf_op jit(solution)/shard_map/scan_rows/pallas_call | solution.py:523
  62.0 2.2 %place_results.1 = (bf16[4,64,1024]{2,1,0:T(8,128)(2,1)}, f32[2,64,1024]{2,1,0:T(8,128)}) custom-call(bf16[4,64,1024]{2,1,0:T(8,128)(2,1)} %get-tuple-element.6.ret_in, f32[2,64,1024]{2,1,0:T(8,128)} %get-tuple-element.7.gb_in), custom_call_target="tpu_custom_call" | custom-call | tf_op jit(solution)/shard_map/place_results/pallas_call | solution.py:585

commit v4 on v3

--- a/solution.py
+++ b/solution.py
@@ -23,7 +23,8 @@
 MODES = 64
 ROWS = 16
 HALF = SEQ // 2
-SECOND = 3
+EARLY = 4
+SECOND = 4
 
 
 def lane_block():
@@ -210,7 +211,10 @@
 
     pack(0)
     pl.semaphore_wait(barrier, SEQ - 1 + DP - 1)
-    launch(0)
+    @pl.when(me >= EARLY)
+    def _():
+        launch(0)
+
     pack(1)
 
     for copy in loads[2 * SETS :]:
@@ -268,6 +272,16 @@
         @pl.when(t != me)
         def _():
             copy_a(c, t, t).wait_recv()
+
+        first = c * SEQ + SEQ - 1 - t
+
+        @pl.when((first == 0) & (me < EARLY))
+        def _():
+            launch(0)
+
+        @pl.when(first == SECOND)
+        def _():
+            launch(1)
 
         for k, dest in enumerate((gd, ud)):
             tile = recv_a[c, t, k * QUARTER : (k + 1) * QUARTER, :].astype(F32)
@@ -408,10 +422,6 @@
         c = n // SEQ
         t = SEQ - 1 - lax.rem(n, SEQ)
 
-        @pl.when(n == SECOND)
-        def _():
-            launch(1)
-
         @pl.when(n == SEQ)
         def _():
             sum_own(0)
@@ -456,10 +466,6 @@
         @pl.when(last == SEQ - 3)
         def _():
             deliver(0)
-
-        @pl.when((last == SEQ - 2) & (me >= HALF))
-        def _():
-            deliver(1)
 
         return 0
 
@@ -468,9 +474,7 @@
     to_sibling(0)
     sum_rows(1)
 
-    @pl.when(me < HALF)
-    def _():
-        deliver(1)
+    deliver(1)
 
     to_sibling(1)
     write_sums(0)

time: 64.3 us -> 59.8 us (0.930)
  Pallas kernels: 63.6 us -> 59 us
    pallas_call x1, Pallas kernels: 61.3 us -> 56.8 us  [shards(): pl.pallas_call(kernel, out_shape=(jax.ShapeDtypeStruct((DP, 64, SETS * WI...]
where the time goes in v4:
time: 59.8 us; the launch traced here: 59.6 us
  Pallas kernels  59 us (99%)
  between operations  0.64 us (1%)
    pallas_call x1, Pallas kernels, shards(): pl.pallas_call(kernel, out_shape=(jax.ShapeDtypeStruct((DP, 64, SETS * WI...  56.8 us
    pallas_call x1, Pallas kernels, shards(): pl.pallas_call(place_kernel, out_shape=(jax.ShapeDtypeStruct(returned.sha...  2.21 us

profile of v4, /device:TPU:1, one launch (start us, length us, event | category | flops | bytes accessed | tf_op | source)
XLA Modules:
  0.0 59.6 jit_solution(12529603266899320286)
XLA Ops:
  0.6 56.8 %scan_rows.1 = (bf16[4,64,1024]{2,1,0:T(8,128)(2,1)}, f32[2,64,1024]{2,1,0:T(8,128)}) custom-call(bf16[1,128,1024]{2,1,0:T(8,128)(2,1)} %grad_hbm.1, bf16[1,128,1024]{2,1,0:T(8,128)(2,1)} %input_hbm.1, f32[64,1024]{1,0:T(8,128)} %decay_hbm.1, f32[64,1024]{1,0:T(8,128)} %freq_hbm.1, f32[2,64,1024]{2,1,0:T(8,128)} %in_hbm.1, f32[2,64,1024]{2,1,0:T(8,128)} %out_hbm.1, ...), custom_call_target="tpu_custom_call" | custom-call | flops 125829120 | bytes 4194304 | tf_op jit(solution)/shard_map/scan_rows/pallas_call | solution.py:527
  57.4 2.2 %place_results.1 = (bf16[4,64,1024]{2,1,0:T(8,128)(2,1)}, f32[2,64,1024]{2,1,0:T(8,128)}) custom-call(bf16[4,64,1024]{2,1,0:T(8,128)(2,1)} %get-tuple-element.6.ret_in, f32[2,64,1024]{2,1,0:T(8,128)} %get-tuple-element.7.gb_in), custom_call_target="tpu_custom_call" | custom-call | tf_op jit(solution)/shard_map/place_results/pallas_call | solution.py:589

commit v5 on v4

--- a/solution.py
+++ b/solution.py
@@ -426,7 +426,7 @@
         def _():
             sum_own(0)
 
-        @pl.when(n == SEQ + 4)
+        @pl.when(n == SEQ + 9)
         def _():
             sum_rows(0)
 
@@ -463,14 +463,11 @@
         def _():
             send_home(1, t)
 
-        @pl.when(last == SEQ - 3)
-        def _():
-            deliver(0)
-
         return 0
 
     lax.fori_loop(0, SETS * SEQ, step, 0)
     sum_own(1)
+    deliver(0)
     to_sibling(0)
     sum_rows(1)
 

time: 59.8 us -> 58.2 us (0.973)
  Pallas kernels: 59 us -> 57.4 us
    pallas_call x1, Pallas kernels: 56.8 us -> 55.2 us  [shards(): pl.pallas_call(kernel, out_shape=(jax.ShapeDtypeStruct((DP, 64, SETS * WI...]
where the time goes in v5:
time: 58.2 us; the launch traced here: 58 us
  Pallas kernels  57.4 us (99%)
  between operations  0.64 us (1%)
    pallas_call x1, Pallas kernels, shards(): pl.pallas_call(kernel, out_shape=(jax.ShapeDtypeStruct((DP, 64, SETS * WI...  55.2 us
    pallas_call x1, Pallas kernels, shards(): pl.pallas_call(place_kernel, out_shape=(jax.ShapeDtypeStruct(returned.sha...  2.21 us

profile of v5, /device:TPU:1, one launch (start us, length us, event | category | flops | bytes accessed | tf_op | source)
XLA Modules:
  0.0 58.0 jit_solution(1650973025107633679)
XLA Ops:
  0.6 55.2 %scan_rows.1 = (bf16[4,64,1024]{2,1,0:T(8,128)(2,1)}, f32[2,64,1024]{2,1,0:T(8,128)}) custom-call(bf16[1,128,1024]{2,1,0:T(8,128)(2,1)} %grad_hbm.1, bf16[1,128,1024]{2,1,0:T(8,128)(2,1)} %input_hbm.1, f32[64,1024]{1,0:T(8,128)} %decay_hbm.1, f32[64,1024]{1,0:T(8,128)} %freq_hbm.1, f32[2,64,1024]{2,1,0:T(8,128)} %in_hbm.1, f32[2,64,1024]{2,1,0:T(8,128)} %out_hbm.1, ...), custom_call_target="tpu_custom_call" | custom-call | flops 125829120 | bytes 4194304 | tf_op jit(solution)/shard_map/scan_rows/pallas_call | solution.py:524
  55.8 2.2 %place_results.1 = (bf16[4,64,1024]{2,1,0:T(8,128)(2,1)}, f32[2,64,1024]{2,1,0:T(8,128)}) custom-call(bf16[4,64,1024]{2,1,0:T(8,128)(2,1)} %get-tuple-element.6.ret_in, f32[2,64,1024]{2,1,0:T(8,128)} %get-tuple-element.7.gb_in), custom_call_target="tpu_custom_call" | custom-call | tf_op jit(solution)/shard_map/place_results/pallas_call | solution.py:586

commit v6 on v5

--- a/solution.py
+++ b/solution.py
@@ -468,8 +468,8 @@
     lax.fori_loop(0, SETS * SEQ, step, 0)
     sum_own(1)
     deliver(0)
+    sum_rows(1)
     to_sibling(0)
-    sum_rows(1)
 
     deliver(1)
 

time: 58.2 us -> 58.2 us (level)
  no operation moved by 1% of the time
where the time goes in v6:
time: 58.2 us; the launch traced here: 58 us
  Pallas kernels  57.4 us (99%)
  between operations  0.64 us (1%)
    pallas_call x1, Pallas kernels, shards(): pl.pallas_call(kernel, out_shape=(jax.ShapeDtypeStruct((DP, 64, SETS * WI...  55.2 us
    pallas_call x1, Pallas kernels, shards(): pl.pallas_call(place_kernel, out_shape=(jax.ShapeDtypeStruct(returned.sha...  2.21 us

profile of v6, /device:TPU:1, one launch (start us, length us, event | category | flops | bytes accessed | tf_op | source)
XLA Modules:
  0.0 58.0 jit_solution(11691695084117312705)
XLA Ops:
  0.6 55.2 %scan_rows.1 = (bf16[4,64,1024]{2,1,0:T(8,128)(2,1)}, f32[2,64,1024]{2,1,0:T(8,128)}) custom-call(bf16[1,128,1024]{2,1,0:T(8,128)(2,1)} %grad_hbm.1, bf16[1,128,1024]{2,1,0:T(8,128)(2,1)} %input_hbm.1, f32[64,1024]{1,0:T(8,128)} %decay_hbm.1, f32[64,1024]{1,0:T(8,128)} %freq_hbm.1, f32[2,64,1024]{2,1,0:T(8,128)} %in_hbm.1, f32[2,64,1024]{2,1,0:T(8,128)} %out_hbm.1, ...), custom_call_target="tpu_custom_call" | custom-call | flops 125829120 | bytes 4194304 | tf_op jit(solution)/shard_map/scan_rows/pallas_call | solution.py:524
  55.8 2.2 %place_results.1 = (bf16[4,64,1024]{2,1,0:T(8,128)(2,1)}, f32[2,64,1024]{2,1,0:T(8,128)}) custom-call(bf16[4,64,1024]{2,1,0:T(8,128)(2,1)} %get-tuple-element.6.ret_in, f32[2,64,1024]{2,1,0:T(8,128)} %get-tuple-element.7.gb_in), custom_call_target="tpu_custom_call" | custom-call | tf_op jit(solution)/shard_map/place_results/pallas_call | solution.py:586
